TPU v7x, 32 devices: a whole 2x2x4 slice. The times are simulated.
32 devices in a mesh: chan: 4 (over y, core), tile: 8 (over z, x).
Axes of the slice: x: 2, y: 2, z: 4, core: 2. Of those that a mesh axis runs over, the one named last changes fastest.
Arguments:
- intensity: bfloat16 [256, 256, 512], P('chan', 'tile'), may hold values from -12 to 12
- block_pick: int32 [8, 4, 4], P('tile', 'chan'), may hold values from 0 to 7, as said below
- owner_tile: int32 [8, 4, 4], P('tile', 'chan'), may hold values from 0 to 7, as said below
- source_index: int32 [8, 4, 4], P('tile', 'chan'), may hold values from 0 to 15
- mask_low: int32 [8, 4, 4, 1024], P('tile', 'chan'), may hold values from 0 to 63
- mask_high: int32 [8, 4, 4, 1024], P('tile', 'chan'), may hold values from 64 to 128
Outputs:
- moment_maps: float32 [8, 4, 8, 2, 1024], P('tile', 'chan')
- spectra: float32 [8, 4, 16, 256], P('tile', 'chan')
- smoothed: bfloat16 [256, 256, 512], P(None, 'tile', 'chan')
Inputs may be any that keep to these rules, and one draw needn't show every extreme that they name: `block_pick`: the 4 block numbers of one device are distinct. `owner_tile`: among the 4 sends of one device no owner appears more than 2 times; in every chan index some owner receives exactly 2 blocks from every device of that chan index.
All inputs are finite; a program needn't handle non-finite values.
Results may differ from a plain program's by a relative error of at most 0.0021.
Values may be sent and summed in bfloat16 or wider, within the bound.
A program may use at most 128 MiB of HBM per device.

v0:
```python
import jax
import jax.numpy as jnp
from jax import lax
from jax.sharding import PartitionSpec as P

BCH = 128
BPIX = 32
RADIUS = 2
CAP = 2
SRC_DEV = 16
SIGMA = 1.5


def with_halo(block, sides, width):
    for axis, dim in sides:
        count = lax.axis_size(axis)
        forward = [(i, i + 1) for i in range(count - 1)]
        backward = [(target, source) for source, target in forward]
        low = lax.ppermute(
            lax.slice_in_dim(block, block.shape[dim] - width, None, axis=dim), axis, forward
        )
        high = lax.ppermute(lax.slice_in_dim(block, 0, width, axis=dim), axis, backward)
        block = jnp.concatenate([low, block, high], axis=dim)
    return block


def gauss_weights():
    offsets = jnp.arange(-RADIUS, RADIUS + 1).astype(jnp.float32)
    raw_weights = jnp.exp(-offsets * offsets / (2.0 * SIGMA * SIGMA))
    return raw_weights / jnp.sum(raw_weights)


def smooth_tiles(framed):
    chan_total = framed.shape[0]
    rows_inner = framed.shape[1] - 2 * RADIUS
    cols_inner = framed.shape[2] - 2 * RADIUS
    chan_blocks = chan_total // BCH
    weights = gauss_weights()

    def smooth_block(block_index):
        first_chan = block_index * BCH
        middle = lax.dynamic_slice_in_dim(framed, first_chan, BCH, 0).astype(jnp.float32)
        before = lax.dynamic_slice_in_dim(framed, jnp.maximum(first_chan - 1, 0), 1, 0).astype(
            jnp.float32
        )
        before = before * (block_index > 0).astype(jnp.float32)
        after = lax.dynamic_slice_in_dim(
            framed, jnp.minimum(first_chan + BCH, chan_total - 1), 1, 0
        ).astype(jnp.float32)
        after = after * (block_index < chan_blocks - 1).astype(jnp.float32)
        lower = jnp.concatenate([before, middle[:-1]], axis=0)
        upper = jnp.concatenate([middle[1:], after], axis=0)
        hanning = 0.5 * middle + 0.25 * (lower + upper)
        row_pass = sum(
            (
                weights[offset] * hanning[:, offset : offset + rows_inner, :]
                for offset in range(2 * RADIUS + 1)
            )
        )
        col_pass = sum(
            (
                weights[offset] * row_pass[:, :, offset : offset + cols_inner]
                for offset in range(2 * RADIUS + 1)
            )
        )
        return col_pass.astype(jnp.bfloat16)

    stacked = lax.map(smooth_block, jnp.arange(chan_blocks, dtype=jnp.int32))
    return stacked.reshape(chan_total, rows_inner, cols_inner)


def per_device(intensity, block_pick, owner_tile, source_index, mask_low, mask_high):
    regrouped = lax.all_to_all(intensity, "chan", split_axis=2, concat_axis=0, tiled=True)
    framed = with_halo(regrouped, (("chan", 2), ("tile", 1)), RADIUS)
    tile_cube = smooth_tiles(framed)
    chan_total, rows_inner, cols_inner = tile_cube.shape
    chan_blocks = chan_total // BCH
    block_rows = rows_inner // BPIX
    block_cols = cols_inner // BPIX
    per_chan_block = block_rows * block_cols
    pixel_count = mask_low.shape[-1]
    picks = block_pick.reshape(-1)
    owners = owner_tile.reshape(-1)
    sources = source_index.reshape(-1)
    send_count = picks.shape[0]
    low_rows = mask_low.reshape(send_count, pixel_count)
    high_rows = mask_high.reshape(send_count, pixel_count)
    chan_of = picks // per_chan_block
    positions = jnp.arange(send_count, dtype=jnp.int32)
    earlier = (positions[None, :] < positions[:, None]) & (owners[None, :] == owners[:, None])
    ranking = jnp.sum(earlier.astype(jnp.int32), axis=1)
    slot_of = owners * CAP + ranking
    peer_count = lax.axis_size("tile")
    slot_total = peer_count * CAP
    filled = slot_of[None, :] == jnp.arange(slot_total, dtype=jnp.int32)[:, None]
    occupied = jnp.any(filled, axis=1)
    sender = jnp.sum(jnp.where(filled, positions[None, :], 0), axis=1)
    tags = jnp.stack([jnp.where(occupied, sources[sender], -1), chan_of[sender]], axis=1).reshape(
        peer_count, CAP, 2
    )
    block_total = chan_blocks * per_chan_block
    low_grid = jnp.zeros((block_total, pixel_count), jnp.int32).at[picks].set(low_rows)
    high_grid = jnp.zeros((block_total, pixel_count), jnp.int32).at[picks].set(high_rows)

    def to_tile(grid):
        shaped = grid.reshape(chan_blocks, block_rows, block_cols, BPIX, BPIX).transpose(
            0, 1, 3, 2, 4
        )
        return shaped.reshape(chan_blocks, 1, rows_inner, cols_inner)

    low_tile = to_tile(low_grid)
    high_tile = to_tile(high_grid)
    cube_blocks = tile_cube.reshape(chan_blocks, BCH, rows_inner, cols_inner)
    chan_pos = jnp.arange(BCH, dtype=jnp.int32).reshape(1, BCH, 1, 1)
    inside = (low_tile <= chan_pos) & (chan_pos < high_tile)
    masked = jnp.where(inside, cube_blocks.astype(jnp.float32), 0.0)
    maps_tile = jnp.sum(masked, axis=1)
    spectra_tile = jnp.sum(
        masked.reshape(chan_blocks, BCH, block_rows, BPIX, block_cols, BPIX), axis=(3, 5)
    )
    all_maps = (
        maps_tile.reshape(chan_blocks, block_rows, BPIX, block_cols, BPIX)
        .transpose(0, 1, 3, 2, 4)
        .reshape(block_total, pixel_count)
    )
    all_spectra = spectra_tile.transpose(0, 2, 3, 1).reshape(block_total, BCH)
    slot_picks = picks[sender]
    maps_slots = jnp.where(occupied[:, None], all_maps[slot_picks], 0.0).reshape(
        peer_count, CAP, pixel_count
    )
    spectra_slots = jnp.where(occupied[:, None], all_spectra[slot_picks], 0.0).reshape(
        peer_count, CAP, BCH
    )
    maps_here, spectra_here, tags_here = (
        lax.all_to_all(maps_slots, "tile", split_axis=0, concat_axis=0, tiled=True),
        lax.all_to_all(spectra_slots, "tile", split_axis=0, concat_axis=0, tiled=True),
        lax.all_to_all(tags, "tile", split_axis=0, concat_axis=0, tiled=True),
    )
    moment_maps = maps_here.reshape(1, 1, peer_count, CAP, pixel_count)
    keys_here = (tags_here[..., 0] * chan_blocks + tags_here[..., 1]).reshape(-1)
    selector = (
        keys_here[None, :] == jnp.arange(SRC_DEV * chan_blocks, dtype=jnp.int32)[:, None]
    ).astype(jnp.float32)
    spectra = jnp.dot(
        selector,
        spectra_here.reshape(-1, BCH),
        precision=lax.Precision.HIGHEST,
        preferred_element_type=jnp.float32,
    )
    return (moment_maps, spectra.reshape(1, 1, SRC_DEV, chan_blocks * BCH), tile_cube)


def solution(mesh):
    return jax.shard_map(
        per_device,
        mesh=mesh,
        in_specs=(
            P("chan", "tile", None),
            P("tile", "chan", None),
            P("tile", "chan", None),
            P("tile", "chan", None),
            P("tile", "chan", None, None),
            P("tile", "chan", None, None),
        ),
        out_specs=(
            P("tile", "chan", None, None, None),
            P("tile", "chan", None, None),
            P(None, "tile", "chan"),
        ),
        check_vma=False,
    )
```

profile of v0, /device:TPU:4, one launch (start us, length us, event | category | flops | bytes accessed | tf_op | source)
XLA Modules:
  0.0 183.7 jit_solution(6895373197032733767)
XLA Ops:
  0.6 8.8 %copy.87 = bf16[64,32,512]{0,1,2:T(8,128)(2,1)} copy(bf16[64,32,512]{2,1,0:T(8,128)(2,1)} %param.8) | data formatting | bytes 4194304 | tf_op args[0]
  9.4 5.9 %reshape.268 = bf16[4,2,131072]{2,1,0:T(2,128)(2,1)} reshape(bf16[512,32,64]{2,1,0:T(8,128)(2,1)} %bitcast.84) | data formatting | bytes 4194304
  15.3 3.7 %all-to-all-start = ((bf16[4,2,131072]{2,1,0:T(2,128)(2,1)}), bf16[4,2,131072]{2,1,0:T(2,128)(2,1)S(1)}, u32[]{:S(2)}, u32[]{:S(2)}) async-start(bf16[4,2,131072]{2,1,0:T(2,128)(2,1)} %reshape.268), calls=%async_computation | async-start | bytes 4194304 | tf_op jit(solution)/shard_map/all_to_all | solution.py:73
  22.3 20.5 %all-to-all-done = bf16[4,2,131072]{2,1,0:T(2,128)(2,1)S(1)} async-done(((bf16[4,2,131072]{2,1,0:T(2,128)(2,1)}), bf16[4,2,131072]{2,1,0:T(2,128)(2,1)S(1)}, u32[]{:S(2)}, u32[]{:S(2)}) %all-to-all-start) | async-done | bytes 2097184 | tf_op jit(solution)/shard_map/all_to_all | solution.py:73
  42.8 6.6 %all-to-all-start.2 = ((s32[8,2,2]{1,2,0:T(2,128)}), s32[8,2,2]{1,2,0:T(2,128)S(1)}, u32[]{:S(2)}, u32[]{:S(2)}) async-start(s32[8,2,2]{1,2,0:T(2,128)} %copy.98), calls=%async_computation.2 | async-start | bytes 16384 | tf_op jit(solution)/shard_map/all_to_all | solution.py:137
  49.4 4.0 %reshape.269 = bf16[512,32,64]{2,1,0:T(8,128)(2,1)} reshape(bf16[4,2,131072]{2,1,0:T(2,128)(2,1)S(1)} %all-to-all-done) | data formatting | bytes 4194304
  53.4 6.8 %copy.102 = bf16[64,32,4,128]{3,2,1,0:T(4,128)(2,1)} copy(bf16[64,32,4,128]{0,1,3,2:T(8,128)(2,1)} %bitcast.83) | data formatting | bytes 4194304 | tf_op jit(solution)/shard_map/all_to_all | solution.py:73
  70.3 3.3 %copy.91 = bf16[256,32,2]{0,1,2:T(8,128)(2,1)S(1)} copy(bf16[256,32,2]{2,1,0:T(8,128)(2,1)} %get-tuple-element.93) | data formatting | bytes 65536 | tf_op jit(solution)/shard_map/slice | solution.py:22
  73.6 3.8 %collective-permute-start.1 = (bf16[256,32,2]{0,1,2:T(8,128)(2,1)S(1)}, bf16[256,32,2]{0,1,2:T(8,128)(2,1)S(1)}, u32[]{:S(2)}, u32[]{:S(2)}) collective-permute-start(bf16[256,32,2]{0,1,2:T(8,128)(2,1)S(1)} %copy.91), channel_id=1, source_target_pairs={{8,0},{16,8},{24,16},{9,1},{17,9},{25,17},{10,2},{18,10},{26,18},{... | collective-permute-start | bytes 98312 | tf_op jit(solution)/shard_map/ppermute | solution.py:22
  78.0 4.2 %copy.92 = bf16[256,32,2]{2,1,0:T(8,128)(2,1)} copy(bf16[256,32,2]{0,1,2:T(8,128)(2,1)S(1)} %collective-permute-done) | data formatting | bytes 65536 | tf_op jit(solution)/shard_map/ppermute | solution.py:19
  82.3 4.2 %copy.93 = bf16[256,32,2]{2,1,0:T(8,128)(2,1)} copy(bf16[256,32,2]{0,1,2:T(8,128)(2,1)S(1)} %collective-permute-done.1) | data formatting | bytes 65536 | tf_op jit(solution)/shard_map/ppermute | solution.py:22
  86.5 4.3 %pad_maximum_fusion = bf16[256,32,132]{2,1,0:T(8,128)(2,1)S(1)} fusion(bf16[256,32,2]{2,1,0:T(8,128)(2,1)} %copy.93, bf16[256,32,128]{2,1,0:T(8,128)(2,1)S(1)} %bitcast.82, bf16[256,32,2]{2,1,0:T(8,128)(2,1)} %copy.92), kind=kLoop, calls=%fused_computation.33 | loop fusion | flops 6488064 | bytes 4325376 | tf_op jit(solution)/shard_map/concatenate | solution.py:23
  93.1 3.9 %collective-permute-start.2 = (bf16[256,2,132]{2,1,0:T(2,128)(2,1)S(1)}, bf16[256,2,132]{2,1,0:T(2,128)(2,1)S(1)}, u32[]{:S(2)}, u32[]{:S(2)}) collective-permute-start(bf16[256,2,132]{2,1,0:T(2,128)(2,1)S(1)} %get-tuple-element.90), channel_id=1, source_target_pairs={{0,1},{1,2},{2,3},{3,4},{4,5},{5,6},{6,7},{8,9},{9,10},{10,11},{11... | collective-permute-start | bytes 405512 | tf_op jit(solution)/shard_map/ppermute | solution.py:19
  101.3 7.6 %copy.95 = bf16[256,32,132]{0,2,1:T(8,128)(2,1)} copy(bf16[256,32,132]{2,1,0:T(8,128)(2,1)} %copy-done.5) | data formatting | bytes 4325376 | tf_op jit(solution)/shard_map/concatenate | solution.py:23
  111.2 38.9 %while.12 = (s32[]{:T(128)}, bf16[2,128,32,128]{1,3,2,0:T(8,128)(2,1)}, f32[5]{0:T(128)S(1)}, s32[2]{0:T(128)S(1)}, bf16[256,36,132]{0,2,1:T(8,128)(2,1)S(1)}, /...) while((s32[]{:T(128)}, ...), condition=%wide.region_6.7_spmd, body=%wide.region_5.6_spmd.sunk | while | flops 14994001 | bytes 46544248 | solution.py:68
  121.4 3.8 %fusion.43 = f32[128,32,132]{0,2,1:T(8,128)S(1)} fusion(f32[128,36,132]{0,2,1:T(8,128)S(1)} %fusion.41, f32[]{:T(128)} %bitcast.74, f32[]{:T(128)} %bitcast.75, f32[]{:T(128)} %bitcast.76, f32[]{:T(128)} %bitcast.77, f32[]{:T(128)} %bitcast.78), kind=kLoop, calls=%fused_computation.13.clone.1 | loop fusion | flops 4866048 | bytes 12976148 | tf_op jit(solution)/shard_map/while/body/eval_jaxpr/add | solution.py:54
  125.3 5.4 %bitcast_dynamic-update-slice_fusion.2 = bf16[2,128,32,128]{1,3,2,0:T(8,128)(2,1)} fusion(bf16[2,128,32,128]{1,3,2,0:T(8,128)(2,1)} %get-tuple-element.158, s32[]{:T(128)} %get-tuple-element.157, f32[128,32,132]{0,2,1:T(8,128)S(1)} %fusion.43, f32[]{:T(128)} %bitcast.74, f32[]{:T(128)} %bitcast.75, f32[]{:T(128)} %bitcast.76, f32[]{:T(128)} %bitcast.77, ...), kind=kLoop, calls=%fused_computation.32.clone.1 | loop fusion | flops 5242880 | bytes 11537408 | tf_op jit(solution)/shard_map/while/body/jit(dynamic_update_index_in_dim)/dynamic_update_slice | solution.py:68
  140.9 3.8 %fusion.43 = f32[128,32,132]{0,2,1:T(8,128)S(1)} fusion(f32[128,36,132]{0,2,1:T(8,128)S(1)} %fusion.41, f32[]{:T(128)} %bitcast.74, f32[]{:T(128)} %bitcast.75, f32[]{:T(128)} %bitcast.76, f32[]{:T(128)} %bitcast.77, f32[]{:T(128)} %bitcast.78), kind=kLoop, calls=%fused_computation.13.clone.1 | loop fusion | flops 4866048 | bytes 12976148 | tf_op jit(solution)/shard_map/while/body/eval_jaxpr/add | solution.py:54
  144.7 5.4 %bitcast_dynamic-update-slice_fusion.2 = bf16[2,128,32,128]{1,3,2,0:T(8,128)(2,1)} fusion(bf16[2,128,32,128]{1,3,2,0:T(8,128)(2,1)} %get-tuple-element.158, s32[]{:T(128)} %get-tuple-element.157, f32[128,32,132]{0,2,1:T(8,128)S(1)} %fusion.43, f32[]{:T(128)} %bitcast.74, f32[]{:T(128)} %bitcast.75, f32[]{:T(128)} %bitcast.76, f32[]{:T(128)} %bitcast.77, ...), kind=kLoop, calls=%fused_computation.32.clone.1 | loop fusion | flops 5242880 | bytes 11537408 | tf_op jit(solution)/shard_map/while/body/jit(dynamic_update_index_in_dim)/dynamic_update_slice | solution.py:68
  150.1 6.1 %fusion.11 = (f32[2,128,128]{1,2,0:T(8,128)S(1)}, f32[2,32,128]{2,1,0:T(8,128)S(1)}) fusion(bf16[2,128,32,128]{1,3,2,0:T(8,128)(2,1)} %get-tuple-element.68, s32[2,32,128]{2,1,0:T(8,128)S(1)} %lt.89, s32[2,32,128]{2,1,0:T(8,128)S(1)} %le.17), kind=kLoop, calls=%fused_computation.35 | loop fusion | flops 7299072 | bytes 2326528 | tf_op jit(solution)/shard_map/reduce_sum | solution.py:118
  157.5 6.6 %all-to-all-start.3 = ((f32[8,2,128]{2,1,0:T(2,128)}), f32[8,2,128]{2,1,0:T(2,128)S(1)}, u32[]{:S(2)}, u32[]{:S(2)}) async-start(f32[8,2,128]{2,1,0:T(2,128)} %broadcast_select_fusion.1), calls=%async_computation.3 | async-start | bytes 16384 | tf_op jit(solution)/shard_map/all_to_all | solution.py:136
  165.7 4.5 %copy.101 = bf16[2,128,32,128]{3,2,1,0:T(8,128)(2,1)} copy(bf16[2,128,32,128]{1,3,2,0:T(8,128)(2,1)} %get-tuple-element.68) | data formatting | bytes 4194304 | tf_op jit(solution)/shard_map/while | solution.py:68
  170.6 5.6 %all-to-all-start.1 = ((f32[8,2,1024]{2,1,0:T(2,128)}), f32[8,2,1024]{2,1,0:T(2,128)S(1)}, u32[]{:S(2)}, u32[]{:S(2)}) async-start(f32[8,2,1024]{2,1,0:T(2,128)} %broadcast_select_fusion), calls=%async_computation.1 | async-start | bytes 131072 | tf_op jit(solution)/shard_map/all_to_all | solution.py:135
  176.9 6.2 %all-to-all-done.1 = f32[8,2,1024]{2,1,0:T(2,128)S(1)} async-done(((f32[8,2,1024]{2,1,0:T(2,128)}), f32[8,2,1024]{2,1,0:T(2,128)S(1)}, u32[]{:S(2)}, u32[]{:S(2)}) %all-to-all-start.1) | async-done | bytes 65568 | tf_op jit(solution)/shard_map/all_to_all | solution.py:135
  (92 shorter events, 43.8 us)
Async XLA Ops:
  0.6 98.4 %copy-start = (s32[1,1,4,1024]{3,2,1,0:T(4,128)S(1)}, s32[1,1,4,1024]{3,2,1,0:T(4,128)}, u32[]{:S(2)}) copy-start(s32[1,1,4,1024]{3,2,1,0:T(4,128)} %param.12) | copy-start | bytes 49156
  15.3 3.8 %copy-start.7 = (s32[1,1,4]{2,1,0:T(1,128)S(1)}, s32[1,1,4]{2,1,0:T(1,128)}, u32[]{:S(2)}) copy-start(s32[1,1,4]{2,1,0:T(1,128)} %param.10) | copy-start | bytes 52
  15.3 4.1 %copy-start.2 = (s32[1,1,4]{2,1,0:T(1,128)S(1)}, s32[1,1,4]{2,1,0:T(1,128)}, u32[]{:S(2)}) copy-start(s32[1,1,4]{2,1,0:T(1,128)} %param.9) | copy-start | bytes 52
  15.3 4.7 %copy-start.1 = (s32[1,1,4]{2,1,0:T(1,128)S(1)}, s32[1,1,4]{2,1,0:T(1,128)}, u32[]{:S(2)}) copy-start(s32[1,1,4]{2,1,0:T(1,128)} %param.11) | copy-start | bytes 52
  15.3 27.5 %all-to-all-start = ((bf16[4,2,131072]{2,1,0:T(2,128)(2,1)}), bf16[4,2,131072]{2,1,0:T(2,128)(2,1)S(1)}, u32[]{:S(2)}, u32[]{:S(2)}) async-start(bf16[4,2,131072]{2,1,0:T(2,128)(2,1)} %reshape.268), calls=%async_computation | async-start | bytes 4194304 | tf_op jit(solution)/shard_map/all_to_all | solution.py:73
  42.8 58.4 %all-to-all-start.2 = ((s32[8,2,2]{1,2,0:T(2,128)}), s32[8,2,2]{1,2,0:T(2,128)S(1)}, u32[]{:S(2)}, u32[]{:S(2)}) async-start(s32[8,2,2]{1,2,0:T(2,128)} %copy.98), calls=%async_computation.2 | async-start | bytes 16384 | tf_op jit(solution)/shard_map/all_to_all | solution.py:137
  68.4 9.7 %collective-permute-start = (bf16[256,32,2]{0,1,2:T(8,128)(2,1)S(1)}, bf16[256,32,2]{0,1,2:T(8,128)(2,1)S(1)}, u32[]{:S(2)}, u32[]{:S(2)}) collective-permute-start(bf16[256,32,2]{0,1,2:T(8,128)(2,1)S(1)} %copy.90), channel_id=1, source_target_pairs={{0,8},{8,16},{16,24},{1,9},{9,17},{17,25},{2,10},{10,18},{18,26},{... | collective-permute-start | bytes 98312 | tf_op jit(solution)/shard_map/ppermute | solution.py:19
  73.6 8.7 %collective-permute-start.1 = (bf16[256,32,2]{0,1,2:T(8,128)(2,1)S(1)}, bf16[256,32,2]{0,1,2:T(8,128)(2,1)S(1)}, u32[]{:S(2)}, u32[]{:S(2)}) collective-permute-start(bf16[256,32,2]{0,1,2:T(8,128)(2,1)S(1)} %copy.91), channel_id=1, source_target_pairs={{8,0},{16,8},{24,16},{9,1},{17,9},{25,17},{10,2},{18,10},{26,18},{... | collective-permute-start | bytes 98312 | tf_op jit(solution)/shard_map/ppermute | solution.py:22
  86.5 13.6 %copy-start.6 = (s32[1,1,4,1024]{3,2,1,0:T(4,128)S(1)}, s32[1,1,4,1024]{3,2,1,0:T(4,128)}, u32[]{:S(2)}) copy-start(s32[1,1,4,1024]{3,2,1,0:T(4,128)} %param.13) | copy-start | bytes 49156
  90.7 1.9 %copy-start.5 = (bf16[256,32,132]{2,1,0:T(8,128)(2,1)}, bf16[256,32,132]{2,1,0:T(8,128)(2,1)S(1)}, u32[]{:S(2)}) copy-start(bf16[256,32,132]{2,1,0:T(8,128)(2,1)S(1)} %pad_maximum_fusion) | copy-start | bytes 6488068
  93.1 15.8 %collective-permute-start.2 = (bf16[256,2,132]{2,1,0:T(2,128)(2,1)S(1)}, bf16[256,2,132]{2,1,0:T(2,128)(2,1)S(1)}, u32[]{:S(2)}, u32[]{:S(2)}) collective-permute-start(bf16[256,2,132]{2,1,0:T(2,128)(2,1)S(1)} %get-tuple-element.90), channel_id=1, source_target_pairs={{0,1},{1,2},{2,3},{3,4},{4,5},{5,6},{6,7},{8,9},{9,10},{10,11},{11... | collective-permute-start | bytes 405512 | tf_op jit(solution)/shard_map/ppermute | solution.py:19
  97.0 12.1 %collective-permute-start.3 = (bf16[256,2,132]{2,1,0:T(2,128)(2,1)S(1)}, bf16[256,2,132]{2,1,0:T(2,128)(2,1)S(1)}, u32[]{:S(2)}, u32[]{:S(2)}) collective-permute-start(bf16[256,2,132]{2,1,0:T(2,128)(2,1)S(1)} %get-tuple-element.91), channel_id=1, source_target_pairs={{1,0},{2,1},{3,2},{4,3},{5,4},{6,5},{7,6},{9,8},{10,9},{11,10},{12... | collective-permute-start | bytes 405512 | tf_op jit(solution)/shard_map/ppermute | solution.py:22
  116.9 1.7 copy-start.3
  117.0 2.5 %copy-start.4 = (f32[1,36,132]{0,2,1:T(8,128)S(1)}, f32[1,36,132]{0,2,1:T(8,128)}, u32[]{:S(2)}) copy-start(f32[1,36,132]{0,2,1:T(8,128)} %get-tuple-element.135) | copy-start | bytes 57028 | tf_op jit(solution)/shard_map/while
  136.4 1.7 copy-start.3
  136.4 2.5 %copy-start.4 = (f32[1,36,132]{0,2,1:T(8,128)S(1)}, f32[1,36,132]{0,2,1:T(8,128)}, u32[]{:S(2)}) copy-start(f32[1,36,132]{0,2,1:T(8,128)} %get-tuple-element.135) | copy-start | bytes 57028 | tf_op jit(solution)/shard_map/while
  157.5 13.1 %all-to-all-start.3 = ((f32[8,2,128]{2,1,0:T(2,128)}), f32[8,2,128]{2,1,0:T(2,128)S(1)}, u32[]{:S(2)}, u32[]{:S(2)}) async-start(f32[8,2,128]{2,1,0:T(2,128)} %broadcast_select_fusion.1), calls=%async_computation.3 | async-start | bytes 16384 | tf_op jit(solution)/shard_map/all_to_all | solution.py:136
  170.6 12.5 %all-to-all-start.1 = ((f32[8,2,1024]{2,1,0:T(2,128)}), f32[8,2,1024]{2,1,0:T(2,128)S(1)}, u32[]{:S(2)}, u32[]{:S(2)}) async-start(f32[8,2,1024]{2,1,0:T(2,128)} %broadcast_select_fusion), calls=%async_computation.1 | async-start | bytes 131072 | tf_op jit(solution)/shard_map/all_to_all | solution.py:135
where the time goes:
time: 185 us; the launch traced here: 184 us
  local copies, waits for them, and re-layouts  75.2 us (41%)
  other arithmetic  42.9 us (23%)
  starting transfers between devices  33.5 us (18%)
  waiting for transfers between devices  27.1 us (15%)
  loops' own time  4.01 us (2%)
    unnamed x16, local copies, waits for them, and re-layouts  21.3 us
    all_to_all x1, waiting for transfers between devices, per_device(): lax.all_to_all(intensity, 'chan', split_axis=2, concat_axis=0, tiled=True)  20.5 us
    dynamic_update_slice x2, other arithmetic, smooth_tiles(): stacked = lax.map(smooth_block, jnp.arange(chan_blocks, dtype=jnp.int32))  10.8 us
    all_to_all x2, local copies, waits for them, and re-layouts, per_device(): lax.all_to_all(intensity, 'chan', split_axis=2, concat_axis=0, tiled=True)  8.72 us
    add x2, other arithmetic, smooth_block(): sum((weights[offset] * hanning[:, offset:offset + rows_inner, :] for offs...  7.64 us
    concatenate x1, local copies, waits for them, and re-layouts, with_halo(): block = jnp.concatenate([low, block, high], axis=dim)  7.57 us
    slice x3, local copies, waits for them, and re-layouts, with_halo(): lax.slice_in_dim(block, block.shape[dim] - width, None, axis=dim)  6.64 us
    all_to_all x1, starting transfers between devices, per_device(): lax.all_to_all(spectra_slots, 'tile', split_axis=0, concat_axis=0, tiled=...  6.62 us
  transfers between devices with their start and end apart: 8, of which 3 were waited for; matrix products, arithmetic and copies ran while one was open for 31% of the time, Pallas kernels for 0%

commit v1 on v0

--- a/solution.py
+++ b/solution.py
@@ -70,7 +70,12 @@
 
 
 def per_device(intensity, block_pick, owner_tile, source_index, mask_low, mask_high):
-    regrouped = lax.all_to_all(intensity, "chan", split_axis=2, concat_axis=0, tiled=True)
+    regrouped = jnp.concatenate(
+        lax.all_to_all(
+            jnp.stack(jnp.split(intensity, lax.axis_size("chan"), axis=2)), "chan", 0, 0
+        ),
+        axis=0,
+    )
     framed = with_halo(regrouped, (("chan", 2), ("tile", 1)), RADIUS)
     tile_cube = smooth_tiles(framed)
     chan_total, rows_inner, cols_inner = tile_cube.shape

time: 185 us -> 161 us (0.87)
  local copies, waits for them, and re-layouts: 75.2 us -> 49.7 us
    unnamed x16 -> x13, local copies, waits for them, and re-layouts: 21.3 us -> 2.58 us
    all_to_all x2 -> x0, local copies, waits for them, and re-layouts: 8.72 us -> none  [per_device(): lax.all_to_all(intensity, 'chan', split_axis=2, concat_axis=0, tiled=True)]
    another operation x0 -> x1, local copies, waits for them, and re-layouts: none -> 1.97 us  [per_device(): jnp.stack(jnp.split(intensity, lax.axis_size('chan'), axis=2))]
  transfers between devices with their start and end apart: 8 -> 8, of which waited for: 3 -> 3; matrix products, arithmetic and copies ran while one was open for 31% -> 27% of each run, Pallas kernels for 0% -> 0%
where the time goes in v1:
time: 161 us; the launch traced here: 159 us
  local copies, waits for them, and re-layouts  49.7 us (31%)
  other arithmetic  44.3 us (28%)
  starting transfers between devices  32.4 us (20%)
  waiting for transfers between devices  28 us (17%)
  loops' own time  4.01 us (2%)
    all_to_all x1, waiting for transfers between devices, per_device(): lax.all_to_all(jnp.stack(jnp.split(intensity, lax.axis_size('chan'), axis...  20.5 us
    dynamic_update_slice x2, other arithmetic, smooth_tiles(): stacked = lax.map(smooth_block, jnp.arange(chan_blocks, dtype=jnp.int32))  10.7 us
    concatenate x1, local copies, waits for them, and re-layouts, with_halo(): block = jnp.concatenate([low, block, high], axis=dim)  7.58 us
    add x2, other arithmetic, smooth_block(): sum((weights[offset] * hanning[:, offset:offset + rows_inner, :] for offs...  7.52 us
    slice x3, local copies, waits for them, and re-layouts, with_halo(): lax.slice_in_dim(block, block.shape[dim] - width, None, axis=dim)  6.63 us
    all_to_all x1, starting transfers between devices, per_device(): lax.all_to_all(spectra_slots, 'tile', split_axis=0, concat_axis=0, tiled=...  6.62 us
    all_to_all x1, starting transfers between devices, per_device(): lax.all_to_all(tags, 'tile', split_axis=0, concat_axis=0, tiled=True)  6.6 us
    concatenate x2, other arithmetic, with_halo(): block = jnp.concatenate([low, block, high], axis=dim)  6.21 us
  transfers between devices with their start and end apart: 8, of which 3 were waited for; matrix products, arithmetic and copies ran while one was open for 27% of the time, Pallas kernels for 0%

profile of v1, /device:TPU:4, one launch (start us, length us, event | category | flops | bytes accessed | tf_op | source)
XLA Modules:
  0.0 159.4 jit_solution(3114971557453487257)
XLA Ops:
  4.2 3.7 %all-to-all-start = ((bf16[4,64,32,128]{3,2,1,0:T(8,128)(2,1)}), bf16[4,64,32,128]{3,2,1,0:T(8,128)(2,1)S(1)}, u32[]{:S(2)}, u32[]{:S(2)}) async-start(bf16[4,64,32,128]{3,2,1,0:T(8,128)(2,1)} %pad_maximum_fusion.2), calls=%async_computation | async-start | bytes 4194304 | tf_op jit(solution)/shard_map/all_to_all | solution.py:74
  11.2 20.5 %all-to-all-done = bf16[4,64,32,128]{3,2,1,0:T(8,128)(2,1)S(1)} async-done(((bf16[4,64,32,128]{3,2,1,0:T(8,128)(2,1)}), bf16[4,64,32,128]{3,2,1,0:T(8,128)(2,1)S(1)}, u32[]{:S(2)}, u32[]{:S(2)}) %all-to-all-start) | async-done | bytes 2097184 | tf_op jit(solution)/shard_map/all_to_all | solution.py:74
  31.7 6.6 %all-to-all-start.2 = ((s32[8,2,2]{1,2,0:T(2,128)}), s32[8,2,2]{1,2,0:T(2,128)S(1)}, u32[]{:S(2)}, u32[]{:S(2)}) async-start(s32[8,2,2]{1,2,0:T(2,128)} %copy.52), calls=%async_computation.2 | async-start | bytes 16384 | tf_op jit(solution)/shard_map/all_to_all | solution.py:142
  38.3 3.0 %fusion.34 = (bf16[256,32,2]{2,1,0:T(8,128)(2,1)}, bf16[256,32,2]{2,1,0:T(8,128)(2,1)}) fusion(bf16[256,32,128]{2,1,0:T(8,128)(2,1)S(1)} %bitcast.85), kind=kLoop, calls=%fused_computation.90 | loop fusion | bytes 131072 | tf_op jit(solution)/shard_map/slice | solution.py:20
  41.2 3.3 %copy.44 = bf16[256,32,2]{0,1,2:T(8,128)(2,1)S(1)} copy(bf16[256,32,2]{2,1,0:T(8,128)(2,1)} %get-tuple-element.92) | data formatting | bytes 65536 | tf_op jit(solution)/shard_map/slice | solution.py:20
  46.4 3.3 %copy.45 = bf16[256,32,2]{0,1,2:T(8,128)(2,1)S(1)} copy(bf16[256,32,2]{2,1,0:T(8,128)(2,1)} %get-tuple-element.93) | data formatting | bytes 65536 | tf_op jit(solution)/shard_map/slice | solution.py:22
  49.7 3.6 %collective-permute-start.1 = (bf16[256,32,2]{0,1,2:T(8,128)(2,1)S(1)}, bf16[256,32,2]{0,1,2:T(8,128)(2,1)S(1)}, u32[]{:S(2)}, u32[]{:S(2)}) collective-permute-start(bf16[256,32,2]{0,1,2:T(8,128)(2,1)S(1)} %copy.45), channel_id=1, source_target_pairs={{8,0},{16,8},{24,16},{9,1},{17,9},{25,17},{10,2},{18,10},{26,18},{... | collective-permute-start | bytes 98312 | tf_op jit(solution)/shard_map/ppermute | solution.py:22
  54.0 4.2 %copy.46 = bf16[256,32,2]{2,1,0:T(8,128)(2,1)} copy(bf16[256,32,2]{0,1,2:T(8,128)(2,1)S(1)} %collective-permute-done) | data formatting | bytes 65536 | tf_op jit(solution)/shard_map/ppermute | solution.py:19
  58.2 4.2 %copy.47 = bf16[256,32,2]{2,1,0:T(8,128)(2,1)} copy(bf16[256,32,2]{0,1,2:T(8,128)(2,1)S(1)} %collective-permute-done.1) | data formatting | bytes 65536 | tf_op jit(solution)/shard_map/ppermute | solution.py:22
  62.4 4.3 %pad_maximum_fusion = bf16[256,32,132]{2,1,0:T(8,128)(2,1)S(1)} fusion(bf16[256,32,2]{2,1,0:T(8,128)(2,1)} %copy.47, bf16[256,32,128]{2,1,0:T(8,128)(2,1)S(1)} %bitcast.86, bf16[256,32,2]{2,1,0:T(8,128)(2,1)} %copy.46), kind=kLoop, calls=%fused_computation.33 | loop fusion | flops 6488064 | bytes 4325376 | tf_op jit(solution)/shard_map/concatenate | solution.py:23
  69.0 3.9 %collective-permute-start.2 = (bf16[256,2,132]{2,1,0:T(2,128)(2,1)S(1)}, bf16[256,2,132]{2,1,0:T(2,128)(2,1)S(1)}, u32[]{:S(2)}, u32[]{:S(2)}) collective-permute-start(bf16[256,2,132]{2,1,0:T(2,128)(2,1)S(1)} %get-tuple-element.90), channel_id=1, source_target_pairs={{0,1},{1,2},{2,3},{3,4},{4,5},{5,6},{6,7},{8,9},{9,10},{10,11},{11... | collective-permute-start | bytes 405512 | tf_op jit(solution)/shard_map/ppermute | solution.py:19
  77.2 7.6 %copy.49 = bf16[256,32,132]{0,2,1:T(8,128)(2,1)} copy(bf16[256,32,132]{2,1,0:T(8,128)(2,1)} %copy-done.5) | data formatting | bytes 4325376 | tf_op jit(solution)/shard_map/concatenate | solution.py:23
  87.1 38.6 %while.12 = (s32[]{:T(128)}, bf16[2,128,32,128]{1,3,2,0:T(8,128)(2,1)}, f32[5]{0:T(128)S(1)}, s32[2]{0:T(128)S(1)}, bf16[256,36,132]{0,2,1:T(8,128)(2,1)S(1)}, /...) while((s32[]{:T(128)}, ...), condition=%wide.region_6.7_spmd, body=%wide.region_5.6_spmd.sunk | while | flops 14994001 | bytes 46544248 | solution.py:68
  89.7 3.0 %convert_multiply_fusion.3 = (f32[1,36,132]{0,2,1:T(8,128)}, f32[1,36,132]{0,2,1:T(8,128)}) fusion(f32[]{:T(128)} %bitcast.76, bf16[256,36,132]{0,2,1:T(8,128)(2,1)S(1)} %get-tuple-element.179, s32[]{:T(128)S(6)} %select_n.117, f32[]{:T(128)} %bitcast.77, s32[]{:T(128)S(6)} %max.7), kind=kLoop, calls=%fused_computation.10.clone.1 | loop fusion | flops 19008 | bytes 57040 | tf_op jit(solution)/shard_map/while/body/eval_jaxpr/mul | solution.py:50
  97.4 3.8 %fusion.43 = f32[128,32,132]{0,2,1:T(8,128)S(1)} fusion(f32[128,36,132]{0,2,1:T(8,128)S(1)} %fusion.41, f32[]{:T(128)} %bitcast.78, f32[]{:T(128)} %bitcast.79, f32[]{:T(128)} %bitcast.80, f32[]{:T(128)} %bitcast.81, f32[]{:T(128)} %bitcast.82), kind=kLoop, calls=%fused_computation.13.clone.1 | loop fusion | flops 4866048 | bytes 12976148 | tf_op jit(solution)/shard_map/while/body/eval_jaxpr/add | solution.py:54
  101.1 5.3 %bitcast_dynamic-update-slice_fusion.2 = bf16[2,128,32,128]{1,3,2,0:T(8,128)(2,1)} fusion(bf16[2,128,32,128]{1,3,2,0:T(8,128)(2,1)} %get-tuple-element.162, s32[]{:T(128)} %get-tuple-element.161, f32[128,32,132]{0,2,1:T(8,128)S(1)} %fusion.43, f32[]{:T(128)} %bitcast.78, f32[]{:T(128)} %bitcast.79, f32[]{:T(128)} %bitcast.80, f32[]{:T(128)} %bitcast.81, ...), kind=kLoop, calls=%fused_computation.32.clone.1 | loop fusion | flops 5242880 | bytes 11537408 | tf_op jit(solution)/shard_map/while/body/jit(dynamic_update_index_in_dim)/dynamic_update_slice | solution.py:68
  109.0 3.0 %convert_multiply_fusion.3 = (f32[1,36,132]{0,2,1:T(8,128)}, f32[1,36,132]{0,2,1:T(8,128)}) fusion(f32[]{:T(128)} %bitcast.76, bf16[256,36,132]{0,2,1:T(8,128)(2,1)S(1)} %get-tuple-element.179, s32[]{:T(128)S(6)} %select_n.117, f32[]{:T(128)} %bitcast.77, s32[]{:T(128)S(6)} %max.7), kind=kLoop, calls=%fused_computation.10.clone.1 | loop fusion | flops 19008 | bytes 57040 | tf_op jit(solution)/shard_map/while/body/eval_jaxpr/mul | solution.py:50
  116.7 3.8 %fusion.43 = f32[128,32,132]{0,2,1:T(8,128)S(1)} fusion(f32[128,36,132]{0,2,1:T(8,128)S(1)} %fusion.41, f32[]{:T(128)} %bitcast.78, f32[]{:T(128)} %bitcast.79, f32[]{:T(128)} %bitcast.80, f32[]{:T(128)} %bitcast.81, f32[]{:T(128)} %bitcast.82), kind=kLoop, calls=%fused_computation.13.clone.1 | loop fusion | flops 4866048 | bytes 12976148 | tf_op jit(solution)/shard_map/while/body/eval_jaxpr/add | solution.py:54
  120.4 5.3 %bitcast_dynamic-update-slice_fusion.2 = bf16[2,128,32,128]{1,3,2,0:T(8,128)(2,1)} fusion(bf16[2,128,32,128]{1,3,2,0:T(8,128)(2,1)} %get-tuple-element.162, s32[]{:T(128)} %get-tuple-element.161, f32[128,32,132]{0,2,1:T(8,128)S(1)} %fusion.43, f32[]{:T(128)} %bitcast.78, f32[]{:T(128)} %bitcast.79, f32[]{:T(128)} %bitcast.80, f32[]{:T(128)} %bitcast.81, ...), kind=kLoop, calls=%fused_computation.32.clone.1 | loop fusion | flops 5242880 | bytes 11537408 | tf_op jit(solution)/shard_map/while/body/jit(dynamic_update_index_in_dim)/dynamic_update_slice | solution.py:68
  125.8 6.1 %fusion.11 = (f32[2,128,128]{1,2,0:T(8,128)S(1)}, f32[2,32,128]{2,1,0:T(8,128)S(1)}) fusion(bf16[2,128,32,128]{1,3,2,0:T(8,128)(2,1)} %get-tuple-element.68, s32[2,32,128]{2,1,0:T(8,128)S(1)} %lt.89, s32[2,32,128]{2,1,0:T(8,128)S(1)} %le.17), kind=kLoop, calls=%fused_computation.35 | loop fusion | flops 7299072 | bytes 2326528 | tf_op jit(solution)/shard_map/reduce_sum | solution.py:123
  134.0 6.6 %all-to-all-start.3 = ((f32[8,2,128]{2,1,0:T(2,128)}), f32[8,2,128]{2,1,0:T(2,128)S(1)}, u32[]{:S(2)}, u32[]{:S(2)}) async-start(f32[8,2,128]{2,1,0:T(2,128)} %broadcast_select_fusion.1), calls=%async_computation.3 | async-start | bytes 16384 | tf_op jit(solution)/shard_map/all_to_all | solution.py:141
  141.4 4.5 %copy.55 = bf16[2,128,32,128]{3,2,1,0:T(8,128)(2,1)} copy(bf16[2,128,32,128]{1,3,2,0:T(8,128)(2,1)} %get-tuple-element.68) | data formatting | bytes 4194304 | tf_op jit(solution)/shard_map/while | solution.py:68
  147.2 4.7 %all-to-all-start.1 = ((f32[8,2,1024]{2,1,0:T(2,128)}), f32[8,2,1024]{2,1,0:T(2,128)S(1)}, u32[]{:S(2)}, u32[]{:S(2)}) async-start(f32[8,2,1024]{2,1,0:T(2,128)} %broadcast_select_fusion), calls=%async_computation.1 | async-start | bytes 131072 | tf_op jit(solution)/shard_map/all_to_all | solution.py:140
  152.6 6.2 %all-to-all-done.1 = f32[8,2,1024]{2,1,0:T(2,128)S(1)} async-done(((f32[8,2,1024]{2,1,0:T(2,128)}), f32[8,2,1024]{2,1,0:T(2,128)S(1)}, u32[]{:S(2)}, u32[]{:S(2)}) %all-to-all-start.1) | async-done | bytes 65568 | tf_op jit(solution)/shard_map/all_to_all | solution.py:140
  (89 shorter events, 34.1 us)
Async XLA Ops:
  0.6 74.4 %copy-start = (s32[1,1,4,1024]{3,2,1,0:T(4,128)S(1)}, s32[1,1,4,1024]{3,2,1,0:T(4,128)}, u32[]{:S(2)}) copy-start(s32[1,1,4,1024]{3,2,1,0:T(4,128)} %param.12) | copy-start | bytes 49156
  4.2 3.7 %copy-start.7 = (s32[1,1,4]{2,1,0:T(1,128)S(1)}, s32[1,1,4]{2,1,0:T(1,128)}, u32[]{:S(2)}) copy-start(s32[1,1,4]{2,1,0:T(1,128)} %param.10) | copy-start | bytes 52
  4.2 4.0 %copy-start.2 = (s32[1,1,4]{2,1,0:T(1,128)S(1)}, s32[1,1,4]{2,1,0:T(1,128)}, u32[]{:S(2)}) copy-start(s32[1,1,4]{2,1,0:T(1,128)} %param.9) | copy-start | bytes 52
  4.2 4.7 %copy-start.1 = (s32[1,1,4]{2,1,0:T(1,128)S(1)}, s32[1,1,4]{2,1,0:T(1,128)}, u32[]{:S(2)}) copy-start(s32[1,1,4]{2,1,0:T(1,128)} %param.11) | copy-start | bytes 52
  4.2 27.5 %all-to-all-start = ((bf16[4,64,32,128]{3,2,1,0:T(8,128)(2,1)}), bf16[4,64,32,128]{3,2,1,0:T(8,128)(2,1)S(1)}, u32[]{:S(2)}, u32[]{:S(2)}) async-start(bf16[4,64,32,128]{3,2,1,0:T(8,128)(2,1)} %pad_maximum_fusion.2), calls=%async_computation | async-start | bytes 4194304 | tf_op jit(solution)/shard_map/all_to_all | solution.py:74
  31.7 45.4 %all-to-all-start.2 = ((s32[8,2,2]{1,2,0:T(2,128)}), s32[8,2,2]{1,2,0:T(2,128)S(1)}, u32[]{:S(2)}, u32[]{:S(2)}) async-start(s32[8,2,2]{1,2,0:T(2,128)} %copy.52), calls=%async_computation.2 | async-start | bytes 16384 | tf_op jit(solution)/shard_map/all_to_all | solution.py:142
  44.5 9.5 %collective-permute-start = (bf16[256,32,2]{0,1,2:T(8,128)(2,1)S(1)}, bf16[256,32,2]{0,1,2:T(8,128)(2,1)S(1)}, u32[]{:S(2)}, u32[]{:S(2)}) collective-permute-start(bf16[256,32,2]{0,1,2:T(8,128)(2,1)S(1)} %copy.44), channel_id=1, source_target_pairs={{0,8},{8,16},{16,24},{1,9},{9,17},{17,25},{2,10},{10,18},{18,26},{... | collective-permute-start | bytes 98312 | tf_op jit(solution)/shard_map/ppermute | solution.py:19
  49.7 8.5 %collective-permute-start.1 = (bf16[256,32,2]{0,1,2:T(8,128)(2,1)S(1)}, bf16[256,32,2]{0,1,2:T(8,128)(2,1)S(1)}, u32[]{:S(2)}, u32[]{:S(2)}) collective-permute-start(bf16[256,32,2]{0,1,2:T(8,128)(2,1)S(1)} %copy.45), channel_id=1, source_target_pairs={{8,0},{16,8},{24,16},{9,1},{17,9},{25,17},{10,2},{18,10},{26,18},{... | collective-permute-start | bytes 98312 | tf_op jit(solution)/shard_map/ppermute | solution.py:22
  62.4 13.6 %copy-start.6 = (s32[1,1,4,1024]{3,2,1,0:T(4,128)S(1)}, s32[1,1,4,1024]{3,2,1,0:T(4,128)}, u32[]{:S(2)}) copy-start(s32[1,1,4,1024]{3,2,1,0:T(4,128)} %param.13) | copy-start | bytes 49156
  66.6 1.9 %copy-start.5 = (bf16[256,32,132]{2,1,0:T(8,128)(2,1)}, bf16[256,32,132]{2,1,0:T(8,128)(2,1)S(1)}, u32[]{:S(2)}) copy-start(bf16[256,32,132]{2,1,0:T(8,128)(2,1)S(1)} %pad_maximum_fusion) | copy-start | bytes 6488068
  69.0 15.8 %collective-permute-start.2 = (bf16[256,2,132]{2,1,0:T(2,128)(2,1)S(1)}, bf16[256,2,132]{2,1,0:T(2,128)(2,1)S(1)}, u32[]{:S(2)}, u32[]{:S(2)}) collective-permute-start(bf16[256,2,132]{2,1,0:T(2,128)(2,1)S(1)} %get-tuple-element.90), channel_id=1, source_target_pairs={{0,1},{1,2},{2,3},{3,4},{4,5},{5,6},{6,7},{8,9},{9,10},{10,11},{11... | collective-permute-start | bytes 405512 | tf_op jit(solution)/shard_map/ppermute | solution.py:19
  72.9 12.0 %collective-permute-start.3 = (bf16[256,2,132]{2,1,0:T(2,128)(2,1)S(1)}, bf16[256,2,132]{2,1,0:T(2,128)(2,1)S(1)}, u32[]{:S(2)}, u32[]{:S(2)}) collective-permute-start(bf16[256,2,132]{2,1,0:T(2,128)(2,1)S(1)} %get-tuple-element.91), channel_id=1, source_target_pairs={{1,0},{2,1},{3,2},{4,3},{5,4},{6,5},{7,6},{9,8},{10,9},{11,10},{12... | collective-permute-start | bytes 405512 | tf_op jit(solution)/shard_map/ppermute | solution.py:22
  92.9 1.7 %copy-start.3 = (f32[1,36,132]{0,2,1:T(8,128)S(1)}, f32[1,36,132]{0,2,1:T(8,128)}, u32[]{:S(2)}) copy-start(f32[1,36,132]{0,2,1:T(8,128)} %get-tuple-element.140) | copy-start | bytes 57028 | tf_op jit(solution)/shard_map/while
  92.9 2.5 %copy-start.4 = (f32[1,36,132]{0,2,1:T(8,128)S(1)}, f32[1,36,132]{0,2,1:T(8,128)}, u32[]{:S(2)}) copy-start(f32[1,36,132]{0,2,1:T(8,128)} %get-tuple-element.139) | copy-start | bytes 57028 | tf_op jit(solution)/shard_map/while
  112.2 1.7 %copy-start.3 = (f32[1,36,132]{0,2,1:T(8,128)S(1)}, f32[1,36,132]{0,2,1:T(8,128)}, u32[]{:S(2)}) copy-start(f32[1,36,132]{0,2,1:T(8,128)} %get-tuple-element.140) | copy-start | bytes 57028 | tf_op jit(solution)/shard_map/while
  112.2 2.5 %copy-start.4 = (f32[1,36,132]{0,2,1:T(8,128)S(1)}, f32[1,36,132]{0,2,1:T(8,128)}, u32[]{:S(2)}) copy-start(f32[1,36,132]{0,2,1:T(8,128)} %get-tuple-element.139) | copy-start | bytes 57028 | tf_op jit(solution)/shard_map/while
  134.0 13.1 %all-to-all-start.3 = ((f32[8,2,128]{2,1,0:T(2,128)}), f32[8,2,128]{2,1,0:T(2,128)S(1)}, u32[]{:S(2)}, u32[]{:S(2)}) async-start(f32[8,2,128]{2,1,0:T(2,128)} %broadcast_select_fusion.1), calls=%async_computation.3 | async-start | bytes 16384 | tf_op jit(solution)/shard_map/all_to_all | solution.py:141
  147.2 11.6 %all-to-all-start.1 = ((f32[8,2,1024]{2,1,0:T(2,128)}), f32[8,2,1024]{2,1,0:T(2,128)S(1)}, u32[]{:S(2)}, u32[]{:S(2)}) async-start(f32[8,2,1024]{2,1,0:T(2,128)} %broadcast_select_fusion), calls=%async_computation.1 | async-start | bytes 131072 | tf_op jit(solution)/shard_map/all_to_all | solution.py:140
